TPU v7x, 32 devices: a whole 2x2x4 slice. The times are simulated.
32 devices in a mesh: pairs: 8 (over z, y), tensor: 4 (over x, core).
Axes of the slice: x: 2, y: 2, z: 4, core: 2. Of those that a mesh axis runs over, the one named last changes fastest.
Arguments:
- queries: bfloat16 [2048, 4096], P('pairs', 'tensor'), may hold values from -100 to 100
- key_rows: bfloat16 [2048, 4096], P('pairs', 'tensor'), may hold values from -3.5 to 3.5
- value_rows: bfloat16 [2048, 4096], P('pairs', 'tensor'), may hold values from -12 to 12
- pair_ids: int32 [2048], P('pairs'), may hold values from 0 to 8, as said below
- out_weight: bfloat16 [4096, 4096], P('tensor', 'pairs'), may hold values from -0.09375 to 0.09375
- residual: bfloat16 [1536, 4096], P('pairs', 'tensor'), may hold values from -6 to 6
Outputs:
- hidden_out: bfloat16 [1536, 4096], P('pairs', 'tensor')
Inputs may be any that keep to these rules, and one draw needn't show every extreme that they name: `pair_ids`: within each block of 256 rows the entries never fall; rows with a value below 8 come first and rows with value 8 form the block's tail; equal values below 8 form one pair. The used rows of blocks 2k and 2k + 1 together number at most 384, reached by some two blocks, and some block has no unused row.
All inputs are finite; a program needn't handle non-finite values.
Results may differ from a plain program's by a relative error of at most 0.0055.
Values may be sent and summed in bfloat16 or wider, within the bound.
A program may use at most 64 MiB of HBM per device.

v0:
```python
import jax
import jax.numpy as jnp
from jax import lax
from jax.sharding import PartitionSpec as P

HEAD = 64
SLOTS = 8


def carried_in(part, axis, combine, identity):
    place = lax.axis_index(axis)
    gathered = lax.all_gather(part, axis)
    state = jnp.zeros_like(part) + jnp.asarray(identity, part.dtype)

    def one(step, state):
        return combine(state, lax.dynamic_index_in_dim(gathered, step, 0, False))

    return lax.fori_loop(0, place, one, state)


def attend_group(query_part, key_part, value_part, allowed):
    scores = jnp.einsum("qhd,khd->hqk", query_part, key_part, preferred_element_type=jnp.float32)
    masked = jnp.where(allowed[None], scores, -1e30)
    row_top = jnp.max(masked, axis=2, keepdims=True)
    exp_terms = jnp.where(allowed[None], jnp.exp(masked - row_top), 0.0)
    row_total = jnp.maximum(jnp.sum(exp_terms, axis=2, keepdims=True), 1.0)
    weights = (exp_terms / row_total).astype(jnp.bfloat16)
    mixed = jnp.einsum("hqk,khd->qhd", weights, value_part, preferred_element_type=jnp.float32)
    return mixed.astype(jnp.bfloat16)


def add_counts(earlier, later):
    return earlier + later


def shards(queries, key_rows, value_rows, pair_ids, out_weight, residual):
    cap_rows = queries.shape[0]
    local_width = queries.shape[1]
    heads_local = local_width // HEAD
    group_size = 4
    balanced_rows = residual.shape[0]
    allowed = (pair_ids[:, None] == pair_ids[None, :]) & (pair_ids[:, None] < SLOTS)

    def split_heads(stacked):
        return stacked.reshape(cap_rows, heads_local // group_size, group_size, HEAD).transpose(
            1, 0, 2, 3
        )

    def per_group(operands):
        return attend_group(operands[0], operands[1], operands[2], allowed)

    grouped = lax.map(
        per_group, (split_heads(queries), split_heads(key_rows), split_heads(value_rows))
    )
    attended = grouped.transpose(1, 0, 2, 3).reshape(cap_rows, local_width)
    live_rows = jnp.sum((pair_ids < SLOTS).astype(jnp.int32))
    devices = lax.axis_size("pairs")
    row_start = carried_in(live_rows.reshape(1), "pairs", add_counts, jnp.zeros((1,), jnp.int32))[0]
    partial_value = jnp.dot(
        attended,
        lax.all_gather(out_weight, "pairs", axis=1, tiled=True),
        preferred_element_type=jnp.float32,
    )
    payload = lax.psum_scatter(
        partial_value.astype(jnp.bfloat16), "tensor", scatter_dimension=1, tiled=True
    )
    per_peer = cap_rows // devices
    feature_width = payload.shape[1]
    peer_index = jnp.arange(devices, dtype=jnp.int32)
    turn_index = jnp.arange(per_peer, dtype=jnp.int32)
    source_rows = ((peer_index - row_start) % devices)[:, None] + devices * turn_index[None, :]
    slot_index = jnp.where(
        source_rows < live_rows, (row_start + source_rows) // devices, balanced_rows
    ).astype(jnp.int32)
    outgoing = jnp.take(payload, source_rows.reshape(-1), axis=0).reshape(
        devices, per_peer, feature_width
    )
    incoming = lax.all_to_all(outgoing, "pairs", split_axis=0, concat_axis=0, tiled=True)
    incoming_slots = lax.all_to_all(slot_index, "pairs", split_axis=0, concat_axis=0, tiled=True)
    landed = jnp.zeros((balanced_rows, feature_width), payload.dtype)
    moved_rows = landed.at[incoming_slots.reshape(-1)].set(
        incoming.reshape(-1, feature_width), mode="drop"
    )
    return (residual.astype(jnp.float32) + moved_rows.astype(jnp.float32)).astype(jnp.bfloat16)


def solution(mesh):
    in_specs = (
        P("pairs", "tensor"),
        P("pairs", "tensor"),
        P("pairs", "tensor"),
        P("pairs"),
        P("tensor", "pairs"),
        P("pairs", "tensor"),
    )
    out_specs = P("pairs", "tensor")
    return jax.shard_map(shards, mesh=mesh, in_specs=in_specs, out_specs=out_specs, check_vma=False)
```

profile of v0, /device:TPU:0, one launch (start us, length us, event | category | flops | bytes accessed | tf_op | source)
XLA Modules:
  0.0 207.7 jit_solution(14955875327928761504)
XLA Ops:
  6.5 0.0 all-gather.2.cloned.1.call-start
  6.5 0.7 all-gather.2.cloned.1.call-update
  7.3 0.0 reduce-scatter.2.cloned.1.call-start
  7.3 1.2 copy.16
  8.6 1.2 copy.17
  9.8 1.2 copy.18
  11.1 1.4 convert_reduce_fusion
  12.4 9.2 %while.22 = (s32[]{:T(128)}, bf16[4,256,4,64]{1,3,2,0:T(8,128)(2,1)S(1)}, bf16[4,256,4,64]{1,3,2,0:T(8,128)(2,1)S(1)}, bf16[4,256,4,64]{1,3,2,0:T(8,128)(2,1)S(1...) while((s32[]{:T(128)}, ...), condition=%wide.region_6.7_spmd.clone, body=%wide.region_3.6_spmd.clone.sunk | while | flops 103221760 | bytes 1134941 | solution.py:52
  12.4 0.9 compare_and_fusion.3
  13.3 0.6 fusion.64
  13.9 0.8 fusion.65
  14.7 0.9 compare_and_fusion.3
  15.6 0.6 fusion.64
  16.2 0.8 fusion.65
  17.0 0.9 compare_and_fusion.3
  17.9 0.6 fusion.64
  18.5 0.8 fusion.65
  19.3 0.9 compare_and_fusion.3
  20.2 0.6 fusion.64
  20.8 0.8 fusion.65
  21.6 0.0 copy-start.1
  21.7 116.0 %all-gather.2.cloned.1.call-done = bf16[1024,4096]{1,0:T(8,128)(2,1)} async-done(((bf16[1024,512]{1,0:T(8,128)(2,1)}), bf16[1024,4096]{1,0:T(8,128)(2,1)}) %all-gather.2.cloned.1.call-update) | async-done | bytes 8388624 | tf_op jit(solution)/shard_map/all_gather | solution.py:61
  137.7 0.0 copy-start
  137.7 7.2 %convolution_convert_fusion.1 = bf16[256,4096]{1,0:T(8,128)(2,1)} fusion(bf16[256,1024]{0,1:T(8,128)(2,1)S(1)} %bitcast.73, bf16[1024,4096]{1,0:T(8,128)(2,1)} %all-gather.2.cloned.1.call-done), kind=kOutput, calls=%fused_computation.29 | convolution fusion | flops 2148532224 | bytes 11010048 | tf_op jit(solution)/shard_map/dot_general | solution.py:59
  144.9 0.0 reduce-scatter.2.cloned.1.call-update
  144.9 0.0 copy-done.1
  144.9 0.6 dynamic-slice
  145.5 1.4 dynamic-update-slice
  146.9 9.5 %all-reduce = s32[8]{0:T(128)S(1)} all-reduce(s32[8]{0:T(128)S(1)} %dynamic-update-slice), channel_id=1, replica_groups=mesh['pairs'=8,'tensor'=4] {'pairs'}, use_global_device_ids=true, to_apply=%add | all-reduce | flops 8 | bytes 64
  156.4 1.4 compare_select_fusion
  157.7 12.8 %all-to-all-start = ((s32[8,1,32]{2,1,0:T(1,128)}), s32[8,1,32]{2,1,0:T(1,128)S(1)}, u32[]{:S(2)}, u32[]{:S(2)}) async-start(s32[8,1,32]{2,1,0:T(1,128)} %compare_select_fusion), calls=%async_computation | async-start | bytes 8192 | tf_op jit(solution)/shard_map/all_to_all | solution.py:79
  170.5 0.1 broadcast_add_fusion
  170.6 0.1 add.137
  170.7 0.1 compare_and_fusion.1
  170.7 3.9 %reduce-scatter.2.cloned.1.call-done = bf16[256,1024]{1,0:T(8,128)(2,1)} async-done(((bf16[256,4096]{1,0:T(8,128)(2,1)}), bf16[256,1024]{1,0:T(8,128)(2,1)}) %reduce-scatter.2.cloned.1.call-update) | async-done | bytes 524304 | tf_op jit(solution)/shard_map/reduce_scatter | solution.py:64
  174.6 2.7 %gather_fusion = bf16[256,1024]{1,0:T(8,128)(2,1)S(1)} fusion(bf16[256,1024]{1,0:T(8,128)(2,1)} %reduce-scatter.2.cloned.1.call-done, s32[1024]{0:T(1024)S(1)} %pad_clamp_fusion), kind=kCustom, calls=%fused_computation | custom fusion | bytes 1049600 | tf_op jit(solution)/shard_map/jit(_take)/gather | solution.py:75
  177.3 0.9 broadcast_select_fusion
  178.2 0.0 all-to-all-done
  178.2 5.5 %all-to-all-start.1 = ((bf16[8,32,1024]{2,1,0:T(8,128)(2,1)}), bf16[8,32,1024]{2,1,0:T(8,128)(2,1)S(1)}, u32[]{:S(2)}, u32[]{:S(2)}) async-start(bf16[8,32,1024]{2,1,0:T(8,128)(2,1)} %broadcast_select_fusion), calls=%async_computation.2 | async-start | bytes 1048576 | tf_op jit(solution)/shard_map/all_to_all | solution.py:78
  183.8 0.5 broadcast.212
  184.3 0.7 reduce.3
  184.9 0.1 reshape.216
  185.0 13.2 %all-to-all-done.1 = bf16[8,32,1024]{2,1,0:T(8,128)(2,1)S(1)} async-done(((bf16[8,32,1024]{2,1,0:T(8,128)(2,1)}), bf16[8,32,1024]{2,1,0:T(8,128)(2,1)S(1)}, u32[]{:S(2)}, u32[]{:S(2)}) %all-to-all-start.1) | async-done | bytes 524320 | tf_op jit(solution)/shard_map/all_to_all | solution.py:78
  198.2 1.7 scatter_custom_fusion
  200.0 0.0 copy-done
  200.0 0.9 add_convert_fusion
  (12 shorter events, 0.1 us)
Async XLA Ops:
  6.5 131.1 %all-gather.2.cloned.1.call-start = ((), (), s32[]{:S(2)}) async-start(), calls=%async_computation.3 | async-start | bytes 9437184 | tf_op jit(solution)/shard_map/all_gather | solution.py:61
  7.3 167.4 %reduce-scatter.2.cloned.1.call-start = ((), (), s32[]{:S(2)}) async-start(), calls=%async_computation.4 | async-start | bytes 2621440 | tf_op jit(solution)/shard_map/reduce_scatter | solution.py:64
  21.6 123.3 %copy-start.1 = (u32[32]{0:T(128)S(1)}, u32[32]{0:T(128)}, u32[]{:S(2)}) copy-start(u32[32]{0:T(128)} %constant.91) | copy-start | bytes 388
  137.7 62.3 %copy-start = (bf16[192,1024]{1,0:T(8,128)(2,1)S(1)}, bf16[192,1024]{1,0:T(8,128)(2,1)}, u32[]{:S(2)}) copy-start(bf16[192,1024]{1,0:T(8,128)(2,1)} %param.15) | copy-start | bytes 1179652
  157.7 20.5 %all-to-all-start = ((s32[8,1,32]{2,1,0:T(1,128)}), s32[8,1,32]{2,1,0:T(1,128)S(1)}, u32[]{:S(2)}, u32[]{:S(2)}) async-start(s32[8,1,32]{2,1,0:T(1,128)} %compare_select_fusion), calls=%async_computation | async-start | bytes 8192 | tf_op jit(solution)/shard_map/all_to_all | solution.py:79
  178.2 20.0 %all-to-all-start.1 = ((bf16[8,32,1024]{2,1,0:T(8,128)(2,1)}), bf16[8,32,1024]{2,1,0:T(8,128)(2,1)S(1)}, u32[]{:S(2)}, u32[]{:S(2)}) async-start(bf16[8,32,1024]{2,1,0:T(8,128)(2,1)} %broadcast_select_fusion), calls=%async_computation.2 | async-start | bytes 1048576 | tf_op jit(solution)/shard_map/all_to_all | solution.py:78
Sparse Core Ops, SparseCore 0:
  9.4 128.2 all-gather.1
  145.0 29.5 reduce-scatter.1
where the time goes:
time: 208 us
  waiting for transfers between devices  134 us (64%)
  starting transfers between devices  18.3 us (9%)
  between operations  13.5 us (6%)
  matrix products  12.8 us (6%)
  local copies, waits for them, and re-layouts  10.8 us (5%)
  blocking collectives  9.45 us (5%)
  other arithmetic  8.86 us (4%)
    all_gather x1, waiting for transfers between devices, shards(): lax.all_gather(out_weight, 'pairs', axis=1, tiled=True)  116 us
    all_to_all x1, waiting for transfers between devices, shards(): lax.all_to_all(outgoing, 'pairs', split_axis=0, concat_axis=0, tiled=True)  13.2 us
    all_to_all x1, starting transfers between devices, shards(): lax.all_to_all(slot_index, 'pairs', split_axis=0, concat_axis=0, tiled=True)  12.8 us
    unnamed x1, blocking collectives  9.45 us
    dot_general x1, matrix products, shards(): jnp.dot(attended, lax.all_gather(out_weight, 'pairs', axis=1, tiled=True)...  7.2 us
    unnamed x10, local copies, waits for them, and re-layouts  5.76 us
    all_to_all x1, starting transfers between devices, shards(): lax.all_to_all(outgoing, 'pairs', split_axis=0, concat_axis=0, tiled=True)  5.52 us
  transfers between devices with their start and end apart: 4, of which 3 were waited for; matrix products, arithmetic and copies ran while one was open for 11% of the time, Pallas kernels for 0%

commit v1 on v0

--- a/solution.py
+++ b/solution.py
@@ -1,6 +1,10 @@
+import functools
+
 import jax
 import jax.numpy as jnp
 from jax import lax
+from jax.experimental import pallas as pl
+from jax.experimental.pallas import tpu as pltpu
 from jax.sharding import PartitionSpec as P
 
 HEAD = 64
@@ -84,6 +88,430 @@
     return (residual.astype(jnp.float32) + moved_rows.astype(jnp.float32)).astype(jnp.bfloat16)
 
 
+HALVES = 2
+PARTS = 2
+WEIGHT_PIECES = 8
+SPILL = 80
+PAIR_CLASSES = 8
+MESH = pl.DeviceIdType.MESH
+BF16 = jnp.bfloat16
+F32 = jnp.float32
+
+
+def attend_pair(query_pair, key_pair, value_pair, allowed):
+    low = lax.broadcasted_iota(jnp.int32, query_pair.shape, 1) < HEAD
+    zero = jnp.zeros_like(query_pair)
+    mixed = []
+    for query_one in (jnp.where(low, query_pair, zero), jnp.where(low, zero, query_pair)):
+        scores = lax.dot_general(
+            query_one, key_pair, (((1,), (1,)), ((), ())), preferred_element_type=F32
+        )
+        masked = jnp.where(allowed, scores, -1e30)
+        exp_terms = jnp.exp(masked - jnp.max(masked, axis=1, keepdims=True))
+        weights = exp_terms * (1.0 / jnp.sum(exp_terms, axis=1, keepdims=True))
+        mixed.append(jnp.dot(weights.astype(BF16), value_pair, preferred_element_type=F32))
+    return jnp.where(low, mixed[0], mixed[1]).astype(BF16)
+
+
+def class_and_turn(place, per_class):
+    kind = jnp.zeros_like(place)
+    for bound in range(1, PAIR_CLASSES):
+        kind = kind + jnp.where(place >= bound * per_class, 1, 0)
+    return kind, place - per_class * kind
+
+
+def fused_kernel(
+    layers, tensors,
+    q_ref, k_ref, v_ref, ids_ref, w_ref, res_ref, out_ref,
+    count_own, counts, w_full, attended, spilled, rows_all,
+    core_out, core_in, mine, across_out, across_in, kept, summed, final_out, final_in,
+    count_send, count_recv, w_send, w_recv, spill_send, spill_recv,
+    own_send, relay_send, rows_recv, core_send, core_recv, across_send, across_recv,
+    final_send, final_recv,
+):
+    devices = layers * HALVES
+    cap = q_ref.shape[0]
+    width = q_ref.shape[1]
+    half_rows = rows_all.shape[2]
+    part_width = width // PARTS
+    quarter = final_in.shape[2]
+    per_class = half_rows // PAIR_CLASSES
+    both = HALVES * half_rows
+    p = lax.axis_index("pairs")
+    t = lax.axis_index("tensor")
+    z = p // HALVES
+    y = p % HALVES
+    x = t // 2
+    core = t % 2
+    beside = (z * HALVES + 1 - y, t)
+    other_core = (p, x * 2 + 1 - core)
+    other_chip = (p, (1 - x) * 2 + core)
+
+    barrier = pltpu.get_barrier_semaphore()
+    everyone = devices * tensors
+
+    def greet(step, carry):
+        number = lax.rem(p * tensors + t + step, everyone)
+        pl.semaphore_signal(
+            barrier, inc=1, device_id=(number // tensors, number % tensors), device_id_type=MESH
+        )
+        return carry
+
+    lax.fori_loop(1, everyone, greet, 0)
+
+    ids_row = ids_ref[...].astype(F32)
+    live = jnp.sum(jnp.where(ids_row < SLOTS, 1.0, 0.0), axis=1, keepdims=True)
+    own_count = jnp.broadcast_to(live, count_own.shape).astype(jnp.int32)
+    count_own[...] = own_count
+    counts[p] = own_count
+    w_full[y] = w_ref[...]
+    ids_wide = jnp.broadcast_to(ids_row, (cap, cap))
+    allowed = ids_wide == ids_wide.T
+    pl.semaphore_wait(barrier, everyone - 1)
+
+    def remote(src, dst, sent, got, where_to):
+        return pltpu.make_async_remote_copy(
+            src_ref=src, dst_ref=dst, send_sem=sent, recv_sem=got,
+            device_id=where_to, device_id_type=MESH,
+        )
+
+    pending = []
+    for step in range(1, devices):
+        peer = lax.rem(p + step, devices)
+        copy = remote(count_own, counts.at[p], count_send.at[step], count_recv.at[p], (peer, t))
+        copy.start()
+        pending.append(copy)
+
+    piece_rows = w_ref.shape[0] // WEIGHT_PIECES
+
+    def weight_copy(piece, slot):
+        rows = pl.ds(piece * piece_rows, piece_rows)
+        return remote(
+            w_ref.at[rows], w_full.at[slot, rows], w_send.at[piece], w_recv.at[piece], beside
+        )
+
+    def send_weights(first, last):
+        for piece in range(first, last):
+            copy = weight_copy(piece, y)
+            copy.start()
+            pending.append(copy)
+
+    def rows_copy(block, part, sent, layer):
+        here = rows_all.at[block, part]
+        return remote(here, here, sent, rows_recv.at[block, part], (layer * HALVES + y, t))
+
+    spill_from = pl.multiple_of((1 - y) * (cap - SPILL), 16)
+
+    def spill_copy(part):
+        return remote(
+            attended.at[part, pl.ds(spill_from, SPILL)], spilled.at[part],
+            spill_send.at[part], spill_recv.at[part], beside,
+        )
+
+    def attend_part(part):
+        for pair in range(part_width // (2 * HEAD)):
+            lanes = slice(part * part_width + pair * 2 * HEAD, part * part_width + (pair + 1) * 2 * HEAD)
+            attended[part, :, pair * 2 * HEAD:(pair + 1) * 2 * HEAD] = attend_pair(
+                q_ref[:, lanes], k_ref[:, lanes], v_ref[:, lanes], allowed
+            )
+        copy = spill_copy(part)
+        copy.start()
+        pending.append(copy)
+
+    send_weights(0, 1)
+    attend_part(0)
+    send_weights(1, 2)
+
+    for step in range(1, devices):
+        source = lax.rem(p + step, devices)
+        remote(count_own, counts.at[source], count_send.at[0], count_recv.at[source], (source, t)).wait_recv()
+
+    def start_of(block):
+        total = jnp.zeros((1, cap), jnp.int32)
+        for earlier in range(devices):
+            total = total + jnp.where(earlier < block, counts[earlier, 0:1, :], 0)
+        return total
+
+    live_first = counts[HALVES * z, 0:1, :]
+    live_second = counts[HALVES * z + 1, 0:1, :]
+    second_at = both - live_second - ((both - live_first - live_second) & 7)
+    start_pair = start_of(HALVES * z)
+    kind, turn = class_and_turn(lax.broadcasted_iota(jnp.int32, (half_rows, cap), 0), per_class)
+    slot = y * half_rows + ((kind - start_pair) & 7) + 8 * turn
+    column = lax.broadcasted_iota(jnp.int32, (half_rows, cap), 1)
+    row_first = slot
+    row_second = slot - second_at
+    row_own = jnp.where(y == 0, row_first, row_second)
+    row_peer = jnp.where(y == 0, row_second, row_first)
+    live_own = jnp.where(y == 0, live_first, live_second)
+    live_peer = jnp.where(y == 0, live_second, live_first)
+    pick_own = jnp.where((column == row_own) & (column < live_own), 1.0, 0.0).astype(BF16)
+    peer_from = y * (cap - SPILL)
+    pick_peer = jnp.where((column == row_peer - peer_from) & (column + peer_from < live_peer), 1.0, 0.0)
+    pick_peer = pick_peer.astype(BF16)[:, :SPILL]
+
+    def share_part(part):
+        spill_copy(part).wait_recv()
+        packed = jnp.dot(pick_own, attended[part], preferred_element_type=F32)
+        packed = packed + jnp.dot(pick_peer, spilled[part], preferred_element_type=F32)
+        rows_all[z, part] = packed.astype(BF16)
+
+        @pl.when(z < layers - 1)
+        def _():
+            rows_copy(z, part, own_send.at[0, part], z + 1).start()
+
+        @pl.when(z > 0)
+        def _():
+            rows_copy(z, part, own_send.at[1, part], z - 1).start()
+
+    share_part(0)
+    for part in range(1, PARTS):
+        attend_part(part)
+        share_part(part)
+    send_weights(2, WEIGHT_PIECES)
+
+    order = (
+        z,
+        jnp.where(z % 2 == 0, z + 1, z - 1),
+        jnp.where(z < 2, 2, 1),
+        jnp.where(z < 2, 3, 0),
+    )
+    inner = (z > 0) & (z < layers - 1)
+
+    def take_rows(turn_index, relay):
+        block = order[turn_index]
+        onward = jnp.where(block < z, z + 1, z - 1)
+        for part in range(PARTS):
+            copy = rows_copy(block, part, relay_send.at[turn_index, part], onward)
+            copy.wait_recv()
+            if relay:
+                copy.start()
+
+    def take_and_relay(turn_index):
+        @pl.when(inner)
+        def _():
+            take_rows(turn_index, True)
+
+    def take_last(turn_index):
+        @pl.when(jnp.logical_not(inner))
+        def _():
+            take_rows(turn_index, False)
+
+    def partial_of(turn_index, side):
+        block = order[turn_index]
+        total = jnp.zeros((half_rows, w_ref.shape[1]), F32)
+        for part in range(PARTS):
+            total = total + jnp.dot(
+                rows_all[block, part],
+                w_full[side, part * part_width:(part + 1) * part_width, :],
+                preferred_element_type=F32,
+            )
+        return total
+
+    def core_copy(turn_index):
+        return remote(
+            core_out.at[turn_index], core_in.at[turn_index],
+            core_send.at[turn_index], core_recv.at[turn_index], other_core,
+        )
+
+    def across_copy(turn_index):
+        return remote(
+            across_out.at[turn_index], across_in.at[turn_index],
+            across_send.at[turn_index], across_recv.at[turn_index], other_chip,
+        )
+
+    def multiply(turn_index):
+        core_out[turn_index] = partial_of(turn_index, 1 - core).astype(BF16)
+        copy = core_copy(turn_index)
+        copy.start()
+        pending.append(copy)
+        mine[turn_index] = partial_of(turn_index, core).astype(BF16)
+
+    def add_cores(turn_index):
+        core_copy(turn_index).wait_recv()
+        total = mine[turn_index].astype(F32) + core_in[turn_index].astype(F32)
+        left, right = total[:, :quarter], total[:, quarter:]
+        across_out[turn_index] = jnp.where(x == 0, right, left).astype(BF16)
+        kept[turn_index] = jnp.where(x == 0, left, right)
+        copy = across_copy(turn_index)
+        copy.start()
+        pending.append(copy)
+
+    def add_chips(turn_index):
+        across_copy(turn_index).wait_recv()
+        total = kept[turn_index] + across_in[turn_index].astype(F32)
+        summed[:, order[turn_index]] = total.reshape(PAIR_CLASSES, per_class, quarter)
+
+    take_and_relay(1)
+    take_and_relay(2)
+    take_and_relay(3)
+    take_last(1)
+    take_last(2)
+    for piece in range(WEIGHT_PIECES):
+        weight_copy(piece, 1 - y).wait_recv()
+    for turn_index in range(layers - 1):
+        multiply(turn_index)
+        if turn_index > 0:
+            add_cores(turn_index - 1)
+    add_cores(layers - 2)
+    take_last(3)
+    multiply(layers - 1)
+    add_cores(layers - 1)
+    for turn_index in range(layers):
+        add_chips(turn_index)
+
+    final_out[...] = summed[...].reshape(final_out.shape).astype(BF16)
+    source_slot = y * tensors + core * 2 + x
+    to_self = z == t
+
+    def final_copy(step):
+        peer = lax.rem(p + step, devices)
+        return remote(
+            final_out.at[peer], final_in.at[source_slot],
+            final_send.at[step], final_recv.at[source_slot], (peer, z),
+        )
+
+    for step in range(1, devices):
+        copy = final_copy(step)
+        copy.start()
+        pending.append(copy)
+
+    @pl.when(to_self)
+    def _():
+        final_in[source_slot] = final_out[p]
+
+    @pl.when(jnp.logical_not(to_self))
+    def _():
+        final_copy(0).start()
+
+    place_shape = (half_rows, HALVES * layers * per_class)
+    lane = lax.broadcasted_iota(jnp.int32, (1, place_shape[1]), 1)
+    side = jnp.where(lane >= layers * per_class, 1, 0)
+    lane = lane - side * layers * per_class
+    layer = jnp.zeros_like(lane)
+    for bound in range(1, layers):
+        layer = layer + jnp.where(lane >= bound * per_class, 1, 0)
+    lane = lane - layer * per_class
+    spot = jnp.zeros_like(lane) - 1
+    count_width = place_shape[1]
+    for block in range(layers):
+        first = counts[HALVES * block, 0:1, :][:, :count_width]
+        second = counts[HALVES * block + 1, 0:1, :][:, :count_width]
+        begin = start_of(HALVES * block)[:, :count_width]
+        second_from = both - second - ((both - first - second) & 7)
+        where_at = side * half_rows + ((p - begin) & 7) + 8 * lane
+        number = jnp.where(
+            where_at < first, begin + where_at,
+            jnp.where(
+                (where_at >= second_from) & (where_at < second_from + second),
+                begin + first + where_at - second_from, -8,
+            ),
+        )
+        spot = jnp.where(layer == block, number >> 3, spot)
+    place = jnp.where(
+        lax.broadcasted_iota(jnp.int32, place_shape, 0) == spot, 1.0, 0.0
+    ).astype(BF16)
+
+    for half in range(HALVES):
+        for piece in range(tensors):
+            slot_index = half * tensors + piece
+            from_self = (z == t) & (source_slot == slot_index)
+
+            @pl.when(jnp.logical_not(from_self))
+            def _():
+                remote(
+                    final_out.at[0], final_in.at[slot_index], final_send.at[0],
+                    final_recv.at[slot_index], (lax.rem(p + 1, devices), t),
+                ).wait_recv()
+
+    depth = layers * per_class
+    for piece in range(tensors):
+        columns = slice(piece * quarter, (piece + 1) * quarter)
+        moved = res_ref[:, columns].astype(F32)
+        for half in range(HALVES):
+            moved = moved + jnp.dot(
+                place[:, half * depth:(half + 1) * depth],
+                final_in[half * tensors + piece], preferred_element_type=F32,
+            )
+        out_ref[:, columns] = moved.astype(BF16)
+
+    for copy in pending:
+        copy.wait_send()
+    for part in range(PARTS):
+        @pl.when(z < layers - 1)
+        def _():
+            rows_copy(z, part, own_send.at[0, part], z + 1).wait_send()
+
+        @pl.when(z > 0)
+        def _():
+            rows_copy(z, part, own_send.at[1, part], z - 1).wait_send()
+
+    @pl.when(inner)
+    def _():
+        for turn_index in range(1, layers):
+            block = order[turn_index]
+            onward = jnp.where(block < z, z + 1, z - 1)
+            for part in range(PARTS):
+                rows_copy(block, part, relay_send.at[turn_index, part], onward).wait_send()
+
+    @pl.when(jnp.logical_not(to_self))
+    def _():
+        final_copy(0).wait_send()
+
+
+def fused_shards(layers, tensors, queries, key_rows, value_rows, pair_ids, out_weight, residual):
+    devices = layers * HALVES
+    cap, width = queries.shape
+    half_rows = residual.shape[0]
+    columns = out_weight.shape[1]
+    quarter = columns // 2
+    part_width = width // PARTS
+    per_class = half_rows // PAIR_CLASSES
+    depth = layers * per_class
+    dma = pltpu.SemaphoreType.DMA
+    vmem = pltpu.VMEM
+    scratch = [
+        vmem((8, cap), jnp.int32),
+        vmem((devices, 8, cap), jnp.int32),
+        vmem((HALVES, width, columns), BF16),
+        vmem((PARTS, cap, part_width), BF16),
+        vmem((PARTS, SPILL, part_width), BF16),
+        vmem((layers, PARTS, half_rows, part_width), BF16),
+        vmem((layers, half_rows, columns), BF16),
+        vmem((layers, half_rows, columns), BF16),
+        vmem((layers, half_rows, columns), BF16),
+        vmem((layers, half_rows, quarter), BF16),
+        vmem((layers, half_rows, quarter), BF16),
+        vmem((layers, half_rows, quarter), F32),
+        vmem((PAIR_CLASSES, layers, per_class, quarter), F32),
+        vmem((devices, depth, quarter), BF16),
+        vmem((HALVES * tensors, depth, quarter), BF16),
+        dma((devices,)), dma((devices,)),
+        dma((WEIGHT_PIECES,)), dma((WEIGHT_PIECES,)),
+        dma((PARTS,)), dma((PARTS,)),
+        dma((2, PARTS)), dma((layers, PARTS)), dma((layers, PARTS)),
+        dma((layers,)), dma((layers,)),
+        dma((layers,)), dma((layers,)),
+        dma((devices,)), dma((HALVES * tensors,)),
+    ]
+    in_vmem = pl.BlockSpec(memory_space=pltpu.VMEM)
+    return pl.pallas_call(
+        functools.partial(fused_kernel, layers, tensors),
+        out_shape=jax.ShapeDtypeStruct(residual.shape, residual.dtype),
+        in_specs=[in_vmem] * 6,
+        out_specs=in_vmem,
+        scratch_shapes=scratch,
+        compiler_params=pltpu.CompilerParams(
+            collective_id=0, has_side_effects=True, vmem_limit_bytes=48 * 1024 * 1024
+        ),
+    )(queries, key_rows, value_rows, pair_ids.reshape(1, cap), out_weight, residual)
+
+
+def fits_fused(mesh):
+    layers = mesh.shape["pairs"] // HALVES
+    return mesh.shape["tensor"] == 4 and layers == 4
+
+
 def solution(mesh):
     in_specs = (
         P("pairs", "tensor"),
@@ -94,4 +522,7 @@
         P("pairs", "tensor"),
     )
     out_specs = P("pairs", "tensor")
-    return jax.shard_map(shards, mesh=mesh, in_specs=in_specs, out_specs=out_specs, check_vma=False)
+    per_device = shards
+    if fits_fused(mesh):
+        per_device = functools.partial(fused_shards, mesh.shape["pairs"] // HALVES, mesh.shape["tensor"])
+    return jax.shard_map(per_device, mesh=mesh, in_specs=in_specs, out_specs=out_specs, check_vma=False)

time: 208 us -> 65.5 us (0.31)
  the two profiles are of different devices: /device:TPU:0 before, /device:TPU:24 now
where the time goes in v1:
time: 65.5 us; the launch traced here: 64.4 us
  Pallas kernels  57.6 us (88%)
  local copies, waits for them, and re-layouts  6.77 us (10%)
    pallas_call x1, Pallas kernels, fused_shards(): pl.pallas_call(functools.partial(fused_kernel, layers, tensors), out_shap...  57.6 us
    unnamed x13, local copies, waits for them, and re-layouts  6.77 us

profile of v1, /device:TPU:24, one launch (start us, length us, event | category | flops | bytes accessed | tf_op | source)
XLA Modules:
  0.0 64.4 jit_solution(14177034040438088374)
XLA Ops:
  0.0 0.0 copy-start.5
  0.0 0.7 %copy-done.5 = s32[256]{0:T(256)S(1)} copy-done((s32[256]{0:T(256)S(1)}, s32[256]{0:T(256)}, u32[]{:S(2)}) %copy-start.5) | copy-done | bytes 1048
  0.7 0.0 copy-start
  0.7 1.2 %copy-done = bf16[1024,512]{1,0:T(8,128)(2,1)S(1)} copy-done((bf16[1024,512]{1,0:T(8,128)(2,1)S(1)}, bf16[1024,512]{1,0:T(8,128)(2,1)}, u32[]{:S(2)}) %copy-start) | copy-done | bytes 1048600
  1.9 0.0 copy-start.1
  1.9 1.0 %copy-done.1 = bf16[256,1024]{1,0:T(8,128)(2,1)S(1)} copy-done((bf16[256,1024]{1,0:T(8,128)(2,1)S(1)}, bf16[256,1024]{1,0:T(8,128)(2,1)}, u32[]{:S(2)}) %copy-start.1) | copy-done | bytes 524312
  2.9 0.0 copy-start.2
  2.9 1.0 %copy-done.2 = bf16[256,1024]{1,0:T(8,128)(2,1)S(1)} copy-done((bf16[256,1024]{1,0:T(8,128)(2,1)S(1)}, bf16[256,1024]{1,0:T(8,128)(2,1)}, u32[]{:S(2)}) %copy-start.2) | copy-done | bytes 524312
  4.0 0.0 copy-start.3
  4.0 1.0 %copy-done.3 = bf16[256,1024]{1,0:T(8,128)(2,1)S(1)} copy-done((bf16[256,1024]{1,0:T(8,128)(2,1)S(1)}, bf16[256,1024]{1,0:T(8,128)(2,1)}, u32[]{:S(2)}) %copy-start.3) | copy-done | bytes 524312
  5.0 0.0 copy-start.4
  5.0 1.0 %copy-done.4 = bf16[192,1024]{1,0:T(8,128)(2,1)S(1)} copy-done((bf16[192,1024]{1,0:T(8,128)(2,1)S(1)}, bf16[192,1024]{1,0:T(8,128)(2,1)}, u32[]{:S(2)}) %copy-start.4) | copy-done | bytes 393240
  6.0 57.6 %shard_map.64 = bf16[192,1024]{1,0:T(8,128)(2,1)S(1)} custom-call(bf16[256,1024]{1,0:T(8,128)(2,1)S(1)} %copy-done.1, bf16[256,1024]{1,0:T(8,128)(2,1)S(1)} %copy-done.2, bf16[256,1024]{1,0:T(8,128)(2,1)S(1)} %copy-done.3, s32[1,256]{1,0:T(1,128)S(1)} %bitcast.1, bf16[1024,512]{1,0:T(8,128)(2,1)S(1)} %copy-done, bf16[192,1024]{1,0:T(8,128)(2,1)S(1)} %copy-done.4), custom_call_target="tpu_custom_call" | custom-call | tf_op jit(solution)/shard_map/pallas_call | solution.py:498
  63.7 0.7 %copy.8 = bf16[192,1024]{1,0:T(8,128)(2,1)} copy(bf16[192,1024]{1,0:T(8,128)(2,1)S(1)} %shard_map.64) | data formatting | bytes 786432
Async XLA Ops:
  0.0 0.7 %copy-start.5 = (s32[256]{0:T(256)S(1)}, s32[256]{0:T(256)}, u32[]{:S(2)}) copy-start(s32[256]{0:T(256)} %param.9) | copy-start | bytes 3076
  0.7 1.2 %copy-start = (bf16[1024,512]{1,0:T(8,128)(2,1)S(1)}, bf16[1024,512]{1,0:T(8,128)(2,1)}, u32[]{:S(2)}) copy-start(bf16[1024,512]{1,0:T(8,128)(2,1)} %w_ref.1) | copy-start | bytes 3145732
  1.9 1.0 %copy-start.1 = (bf16[256,1024]{1,0:T(8,128)(2,1)S(1)}, bf16[256,1024]{1,0:T(8,128)(2,1)}, u32[]{:S(2)}) copy-start(bf16[256,1024]{1,0:T(8,128)(2,1)} %q_ref.1) | copy-start | bytes 1572868
  2.9 1.0 %copy-start.2 = (bf16[256,1024]{1,0:T(8,128)(2,1)S(1)}, bf16[256,1024]{1,0:T(8,128)(2,1)}, u32[]{:S(2)}) copy-start(bf16[256,1024]{1,0:T(8,128)(2,1)} %k_ref.1) | copy-start | bytes 1572868
  4.0 1.0 %copy-start.3 = (bf16[256,1024]{1,0:T(8,128)(2,1)S(1)}, bf16[256,1024]{1,0:T(8,128)(2,1)}, u32[]{:S(2)}) copy-start(bf16[256,1024]{1,0:T(8,128)(2,1)} %v_ref.1) | copy-start | bytes 1572868
  5.0 1.0 %copy-start.4 = (bf16[192,1024]{1,0:T(8,128)(2,1)S(1)}, bf16[192,1024]{1,0:T(8,128)(2,1)}, u32[]{:S(2)}) copy-start(bf16[192,1024]{1,0:T(8,128)(2,1)} %res_ref.1) | copy-start | bytes 1179652
